TPU v7x, 32 devices: a whole 2x2x4 slice. The times are simulated.
32 devices in a mesh: grp: 2 (over y), ad: 4 (over z), tp: 4 (over x, core).
Axes of the slice: x: 2, y: 2, z: 4, core: 2. Of those that a mesh axis runs over, the one named last changes fastest.
Arguments:
- tokens: bfloat16 [512, 8192], P(('grp', 'ad'), 'tp'), parts along dimension 0, may hold values from -6 to 6
- row_adapter_index: int32 [512], P(('grp', 'ad')), parts along dimension 0, may hold values from 0 to 7, as said below
- adapter_slot_table: int32 [16], P('grp'), parts along dimension 0, may hold values from 0 to 7, as said below
- gate_matrix: bfloat16 [8192, 28672], P('tp', 'ad'), may hold values from -0.0625 to 0.0625
- down_weight_slots: bfloat16 [8, 64, 8192], P('ad', None, 'tp'), may hold values from -0.0625 to 0.0625
- up_weight_slots: bfloat16 [8, 64, 28672], P(None, 'tp', 'ad'), may hold values from -0.75 to 0.75
- slot_scale_table: float32 [8], replicated, may hold values from 0.3 to 3
Outputs:
- gated: bfloat16 [512, 28672], P(('grp', 'tp'), 'ad'), parts along dimension 0
There are 2 independent parts, one for each index of `grp`. A program takes and returns all parts, laid end to end along the dimension named above; an argument that names none is the same for every part. Nothing has to cross between parts.
Inputs may be any that keep to these rules, and one draw needn't show every extreme that they name: A permutation: adapter a is stored at slot adapter_slot_table[a], and slot s belongs to index s // 2 of ad. `row_adapter_index`: at most 128 rows name adapters whose slots belong to one index of ad; in every draw one index has exactly 128.
All inputs are finite; a program needn't handle non-finite values.
Results may differ from a plain program's by a relative error of at most 0.015.
Values may be sent and summed in bfloat16 or wider, within the bound.
A program may use at most 128 MiB of HBM per device.

v0:
```python
import jax
import jax.numpy as jnp
from jax import lax
from jax.sharding import PartitionSpec as P


def per_device(
    tokens,
    row_adapter_index,
    adapter_slot_table,
    gate_matrix,
    down_weight_slots,
    up_weight_slots,
    slot_scale_table,
):
    owners = lax.axis_size("ad")
    here = lax.axis_index("ad")
    adapter_group = lax.axis_index("tp")
    rows_dev = tokens.shape[0]
    total = rows_dev * owners
    owner_result = down_weight_slots.shape[0]
    rank_portion = up_weight_slots.shape[1]
    resident_weights = up_weight_slots.shape[0]
    capacity = min(4, owners // 2) * rows_dev
    feature_width = gate_matrix.shape[1]
    gathered, all_ids = (
        lax.all_gather(tokens, "ad", axis=0, tiled=True),
        lax.all_gather(row_adapter_index, "ad", axis=0, tiled=True),
    )
    slot_equality = (
        all_ids[:, None] == jnp.arange(adapter_slot_table.shape[0], dtype=jnp.int32)[None, :]
    )
    slot_table = jnp.sum(jnp.where(slot_equality, adapter_slot_table[None, :], 0), axis=1)
    slot_hits = (
        slot_table[:, None] == jnp.arange(slot_scale_table.shape[0], dtype=jnp.int32)[None, :]
    )
    row_scales = jnp.sum(jnp.where(slot_hits, slot_scale_table[None, :], 0.0), axis=1)
    owner = slot_table // owner_result
    owner_hot = owner[:, None] == jnp.arange(owners, dtype=jnp.int32)[None, :]
    running = jnp.cumsum(owner_hot.astype(jnp.int32), axis=0) - 1
    position = jnp.sum(jnp.where(owner_hot, running, 0), axis=1)
    place = owner * capacity + position
    target = jnp.where(owner == here, position, capacity)
    picked = (
        jnp.zeros((capacity,), jnp.int32)
        .at[target]
        .set(jnp.arange(total, dtype=jnp.int32), mode="drop")
    )
    live = jnp.zeros((capacity,), jnp.bool_).at[target].set(True, mode="drop")
    local_slot = slot_table[picked] - here * owner_result
    choose = (local_slot[:, None] == jnp.arange(owner_result, dtype=jnp.int32)[None, :]) & live[
        :, None
    ]
    slot_table, row_scales, place, picked, choose = (slot_table, row_scales, place, picked, choose)
    partial_value = jnp.dot(gathered, gate_matrix, preferred_element_type=jnp.float32)
    selected_rows = gathered[picked]
    reduced_rank_output = jnp.einsum(
        "no,hto->nht", selected_rows, down_weight_slots, preferred_element_type=jnp.float32
    )
    owner_terms = jnp.sum(jnp.where(choose[:, :, None], reduced_rank_output, 0.0), axis=1).T
    summed = lax.psum(owner_terms.astype(jnp.bfloat16), "tp").astype(jnp.float32)
    mine = lax.dynamic_slice_in_dim(summed, adapter_group * rank_portion, rank_portion, 0)
    rank_piece = mine.astype(jnp.bfloat16)
    all_ranks = lax.all_gather(rank_piece, "ad", axis=1, tiled=True)
    per_row = jnp.take(all_ranks, place, axis=1).T
    slot_match = slot_table[:, None] == jnp.arange(resident_weights, dtype=jnp.int32)[None, :]
    expanded_output = jnp.where(
        slot_match[:, :, None], per_row[:, None, :], jnp.zeros((), jnp.bfloat16)
    )
    expanded_output = expanded_output.reshape(total, resident_weights * rank_portion)
    delta = jnp.dot(
        expanded_output,
        up_weight_slots.reshape(resident_weights * rank_portion, feature_width),
        preferred_element_type=jnp.float32,
    )
    terms = partial_value + row_scales[:, None] * delta
    return lax.psum_scatter(terms.astype(jnp.bfloat16), "tp", scatter_dimension=0, tiled=True)


def solution(mesh):
    in_specs = (
        P(("grp", "ad"), "tp"),
        P(("grp", "ad")),
        P("grp"),
        P("tp", "ad"),
        P("ad", None, "tp"),
        P(None, "tp", "ad"),
        P(),
    )
    out_specs = P(("grp", "tp"), "ad")
    return jax.shard_map(
        per_device, mesh=mesh, in_specs=in_specs, out_specs=out_specs, check_vma=False
    )
```

profile of v0, /device:TPU:0, one launch (start us, length us, event | category | flops | bytes accessed | tf_op | source)
XLA Modules:
  0.0 137.9 jit_solution(1455313458822157787)
XLA Ops:
  6.5 0.0 copy-start
  6.5 0.0 all-gather.2.cloned.1.call-start
  6.5 0.7 all-gather.2.cloned.1.call-update
  7.3 0.0 reduce-scatter.2.cloned.1.call-start
  7.3 1.2 dynamic-slice
  9.2 0.9 dynamic-update-slice
  10.1 9.9 %all-reduce = s32[256]{0:T(256)S(1)} all-reduce(s32[256]{0:T(256)S(1)} %dynamic-update-slice), channel_id=1, replica_groups=mesh['grp'=2,'ad'=4,'tp'=4] {'ad'}, use_global_device_ids=true, to_apply=%add | all-reduce | flops 256 | bytes 2048
  20.0 0.7 select_reduce_fusion.1
  20.7 1.2 reduce-window.6
  22.0 0.1 slice.14
  22.1 0.1 copy.18
  22.2 0.1 copy.19
  22.3 0.1 add_bitcast_fusion
  22.4 1.4 %scatter_custom_fusion = s32[128]{0:T(128)S(1)} fusion(s32[256]{0:T(256)S(1)} %bitcast.50, s32[256]{0:T(256)S(1)} %iota.28, s32[]{:T(128)} %constant.23.clone.1), kind=kCustom, calls=%fused_computation.54 | custom fusion | bytes 516 | tf_op jit(solution)/shard_map/scatter | solution.py:47
  23.9 1.3 gather_fusion
  25.1 1.5 %scatter_custom_fusion.1 = pred[128]{0:T(512)(128)(4,1)S(1)} fusion(s32[256]{0:T(256)S(1)} %bitcast.51, pred[256]{0:T(512)(128)(4,1)S(1)} %broadcast.281, pred[]{:T(512)} %constant.56.clone.1), kind=kCustom, calls=%fused_computation.51 | custom fusion | bytes 129 | tf_op jit(solution)/shard_map/scatter | solution.py:49
  26.7 0.7 select_reduce_fusion
  27.4 12.2 %all-gather.2.cloned.1.call-done = bf16[256,2048]{1,0:T(8,128)(2,1)} async-done(((bf16[64,2048]{1,0:T(8,128)(2,1)}), bf16[256,2048]{1,0:T(8,128)(2,1)}) %all-gather.2.cloned.1.call-update) | async-done | bytes 1048592 | tf_op jit(solution)/shard_map/all_gather | solution.py:27
  39.6 0.0 copy-start.1
  39.6 2.9 %gather_fusion.1 = bf16[128,2048]{1,0:T(8,128)(2,1)S(1)} fusion(bf16[256,2048]{1,0:T(8,128)(2,1)} %all-gather.2.cloned.1.call-done, s32[1024]{0:T(1024)S(1)} %pad_clamp_fusion.1), kind=kCustom, calls=%fused_computation.1 | custom fusion | bytes 1049088 | tf_op jit(solution)/shard_map/gather | solution.py:56
  42.5 1.4 %fusion.2 = bf16[128,64]{0,1:T(8,128)(2,1)S(1)} fusion(bf16[2,64,2048]{2,1,0:T(8,128)(2,1)} %param.11, bf16[128,2048]{1,0:T(8,128)(2,1)S(1)} %gather_fusion.1, pred[128,2]{0,1:T(4,128)(4,1)S(1)} %compare_and_fusion), kind=kOutput, calls=%fused_computation.10 | convolution fusion | flops 67133440 | bytes 1065216 | tf_op jit(solution)/shard_map/no,hto->nht/dot_general | solution.py:57
  43.9 10.8 %psum.7 = bf16[64,128]{1,0:T(8,128)(2,1)S(1)} all-reduce(bf16[64,128]{1,0:T(8,128)(2,1)S(1)} %bitcast.45), channel_id=1, replica_groups=mesh['grp'=2,'ad'=4,'tp'=4] {'tp'}, use_global_device_ids=true, to_apply=%region_8.9 | all-reduce | flops 8192 | bytes 32768 | tf_op jit(solution)/shard_map/psum | solution.py:61
  54.6 11.9 %all_gather.11 = bf16[16,512]{1,0:T(8,128)(2,1)S(1)} all-gather(bf16[16,128]{1,0:T(8,128)(2,1)S(1)} %convert_convert_fusion), channel_id=1, replica_groups=mesh['grp'=2,'ad'=4,'tp'=4] {'ad'}, dimensions={1}, use_global_device_ids=true | all-gather | bytes 20480 | tf_op jit(solution)/shard_map/all_gather | solution.py:64
  66.5 0.1 copy.20
  66.6 0.9 gather_fusion.2
  67.5 0.1 broadcast_select_fusion
  67.6 0.1 copy.21
  67.7 0.0 copy-done
  67.7 4.1 %fusion = f32[256,7168]{1,0:T(8,128)} fusion(bf16[8,16,7168]{2,1,0:T(8,128)(2,1)S(1)} %copy-done, f32[256]{0:T(256)S(1)} %select_reduce_fusion, pred[256,8]{0,1:T(8,128)(4,1)S(1)} %iota_compare_fusion, bf16[256,16]{0,1:T(8,128)(2,1)S(1)} %copy.21), kind=kOutput, calls=%fused_computation.6 | convolution fusion | flops 471629824 | bytes 9186304 | tf_op jit(solution)/shard_map/dot_general | solution.py:71
  71.8 0.0 copy-done.1
  71.8 19.8 %fusion.1 = bf16[256,7168]{1,0:T(8,128)(2,1)} fusion(f32[256,7168]{1,0:T(8,128)} %fusion, bf16[256,2048]{1,0:T(8,128)(2,1)S(1)} %copy-done.1, bf16[2048,7168]{1,0:T(8,128)(2,1)} %param.10), kind=kOutput, calls=%fused_computation.8 | convolution fusion | flops 7519862784 | bytes 41418752 | tf_op jit(solution)/shard_map/dot_general | solution.py:55
  91.6 0.0 reduce-scatter.2.cloned.1.call-update
  91.6 39.4 %reduce-scatter.2.cloned.1.call-done = bf16[64,7168]{1,0:T(8,128)(2,1)} async-done(((bf16[256,7168]{1,0:T(8,128)(2,1)}), bf16[64,7168]{1,0:T(8,128)(2,1)}) %reduce-scatter.2.cloned.1.call-update) | async-done | bytes 917520 | tf_op jit(solution)/shard_map/reduce_scatter | solution.py:77
  (19 shorter events, 0.2 us)
Async XLA Ops:
  6.5 61.1 %copy-start = (bf16[8,16,7168]{2,1,0:T(8,128)(2,1)S(1)}, bf16[8,16,7168]{2,1,0:T(8,128)(2,1)}, u32[]{:S(2)}) copy-start(bf16[8,16,7168]{2,1,0:T(8,128)(2,1)} %param.12) | copy-start | bytes 5505028
  6.5 33.1 %all-gather.2.cloned.1.call-start = ((), (), s32[]{:S(2)}) async-start(), calls=%async_computation.1 | async-start | bytes 1310720 | tf_op jit(solution)/shard_map/all_gather | solution.py:27
  7.3 123.8 %reduce-scatter.2.cloned.1.call-start = ((), (), s32[]{:S(2)}) async-start(), calls=%async_computation.2 | async-start | bytes 4587520 | tf_op jit(solution)/shard_map/reduce_scatter | solution.py:77
  39.6 32.2 %copy-start.1 = (bf16[256,2048]{1,0:T(8,128)(2,1)S(1)}, bf16[256,2048]{1,0:T(8,128)(2,1)}, u32[]{:S(2)}) copy-start(bf16[256,2048]{1,0:T(8,128)(2,1)} %all-gather.2.cloned.1.call-done) | copy-start | bytes 3145732
Sparse Core Ops, SparseCore 0:
  8.9 30.6 all-gather.1
  91.8 39.2 reduce-scatter.1
where the time goes:
time: 138 us
  waiting for transfers between devices  52.3 us (38%)
  blocking collectives  32.5 us (24%)
  matrix products  25.3 us (18%)
  between operations  14.2 us (10%)
  local copies, waits for them, and re-layouts  10.5 us (8%)
  other arithmetic  3.04 us (2%)
    reduce_scatter x1, waiting for transfers between devices, per_device(): lax.psum_scatter(terms.astype(jnp.bfloat16), 'tp', scatter_dimension=0, t...  39.4 us
    dot_general x1, matrix products, per_device(): jnp.dot(gathered, gate_matrix, preferred_element_type=jnp.float32)  19.8 us
    all_gather x1, waiting for transfers between devices, per_device(): lax.all_gather(tokens, 'ad', axis=0, tiled=True)  12.2 us
    all_gather x1, blocking collectives, per_device(): all_ranks = lax.all_gather(rank_piece, 'ad', axis=1, tiled=True)  11.9 us
    psum x1, blocking collectives, per_device(): lax.psum(owner_terms.astype(jnp.bfloat16), 'tp').astype(jnp.float32)  10.8 us
    unnamed x1, blocking collectives  9.89 us
    dot_general x1, matrix products, per_device(): jnp.dot(expanded_output, up_weight_slots.reshape(resident_weights * rank_...  4.14 us
    gather x1, local copies, waits for them, and re-layouts, per_device(): selected_rows = gathered[picked]  2.89 us
  transfers between devices with their start and end apart: 2, of which 2 were waited for; matrix products, arithmetic and copies ran while one was open for 7% of the time, Pallas kernels for 0%

commit v1 on v0

v1 whole, which is shorter than its diff:
```python
import functools

import jax
import jax.numpy as jnp
from jax import lax
from jax.experimental import pallas as pl
from jax.experimental.pallas import tpu as pltpu
from jax.sharding import PartitionSpec as P

PHASES = 2
CHUNKS = 7
EARLY = 3
MESH = pl.DeviceIdType.MESH
F32 = jnp.float32
BF16 = jnp.bfloat16


def kernel(
    n_ad,
    n_tp,
    tokens,
    ids,
    table,
    scales,
    gate,
    down,
    up,
    out,
    x_all,
    w,
    dn,
    upv,
    acc,
    meta_own,
    meta_in,
    slots,
    scale_cols,
    a_send,
    a_recv,
    b_send,
    b_recv,
    spread,
    expand,
    send1,
    recv1,
    keep,
    send2,
    recv2,
    w_sem,
    local_sem,
    x_ssem,
    x_rsem,
    m_ssem,
    m_rsem,
    a_ssem,
    a_rsem,
    b_ssem,
    b_rsem,
    s1_ssem,
    s1_rsem,
    s2_ssem,
    s2_rsem,
):
    me_ad = lax.axis_index("ad")
    me_tp = lax.axis_index("tp")
    core = lax.rem(me_tp, 2)
    me_x = me_tp // 2
    n_x = n_tp // 2
    rows_dev = tokens.shape[0]
    hp = rows_dev // PHASES
    rows = n_ad * hp
    cw = gate.shape[1] // CHUNKS
    tile = 256 if cw % 256 == 0 else cw
    rank_part = a_recv.shape[2]
    rank = rank_part * n_tp
    owned = down.shape[0] // rank
    n_slots = scales.shape[0]
    per_dest = rows // n_tp
    blocks = n_ad // n_tp

    def cols(j):
        return pl.ds(pl.multiple_of(j * cw, cw), cw)

    def ad_peer(k):
        return {"ad": lax.rem(me_ad + k, n_ad)}

    def tp_peer(k):
        return {"tp": lax.rem(me_tp + k, n_tp)}

    def w_copy(j):
        return pltpu.make_async_copy(gate.at[:, cols(j)], w.at[:, cols(j)], w_sem.at[j])

    dn_copy = pltpu.make_async_copy(down, dn, local_sem.at[0])
    up_copy = pltpu.make_async_copy(up, upv, local_sem.at[1])

    def own_rows(p):
        return x_all.at[p, pl.ds(pl.multiple_of(me_ad * hp, hp), hp)]

    def own_copy(p):
        return pltpu.make_async_copy(
            tokens.at[pl.ds(p * hp, hp)], own_rows(p), local_sem.at[2 + p]
        )

    def x_send(p, k):
        return pltpu.make_async_remote_copy(
            src_ref=tokens.at[pl.ds(p * hp, hp)],
            dst_ref=own_rows(p),
            send_sem=x_ssem.at[p, k - 1],
            recv_sem=x_rsem.at[p, k - 1],
            device_id=ad_peer(k),
            device_id_type=MESH,
        )

    def x_recv(p, k):
        origin = lax.rem(me_ad + n_ad - k, n_ad)
        return pltpu.make_async_remote_copy(
            src_ref=tokens.at[pl.ds(p * hp, hp)],
            dst_ref=x_all.at[p, pl.ds(pl.multiple_of(origin * hp, hp), hp)],
            send_sem=x_ssem.at[p, k - 1],
            recv_sem=x_rsem.at[p, k - 1],
            device_id=ad_peer(k),
            device_id_type=MESH,
        )

    def m_copy(k):
        return pltpu.make_async_remote_copy(
            src_ref=meta_own,
            dst_ref=meta_in.at[k - 1],
            send_sem=m_ssem.at[k - 1],
            recv_sem=m_rsem.at[k - 1],
            device_id=ad_peer(k),
            device_id_type=MESH,
        )

    def a_copy(p, k):
        return pltpu.make_async_remote_copy(
            src_ref=a_send.at[p, lax.rem(me_tp + k, n_tp)],
            dst_ref=a_recv.at[p, k - 1],
            send_sem=a_ssem.at[p, k - 1],
            recv_sem=a_rsem.at[p, k - 1],
            device_id=tp_peer(k),
            device_id_type=MESH,
        )

    def b_copy(p, k):
        return pltpu.make_async_remote_copy(
            src_ref=b_send.at[p],
            dst_ref=b_recv.at[p, k - 1],
            send_sem=b_ssem.at[p, k - 1],
            recv_sem=b_rsem.at[p, k - 1],
            device_id=ad_peer(k),
            device_id_type=MESH,
        )

    def s1_copy(p, j):
        return pltpu.make_async_remote_copy(
            src_ref=send1.at[p, j],
            dst_ref=recv1.at[p, j],
            send_sem=s1_ssem.at[p, j],
            recv_sem=s1_rsem.at[p, j],
            device_id={"tp": me_x * 2 + 1 - core},
            device_id_type=MESH,
        )

    def s2_copy(p, j, k):
        return pltpu.make_async_remote_copy(
            src_ref=send2.at[p, j, k - 1],
            dst_ref=recv2.at[p, j, k - 1],
            send_sem=s2_ssem.at[p, j, k - 1],
            recv_sem=s2_rsem.at[p, j, k - 1],
            device_id={"tp": lax.rem(me_x + k, n_x) * 2 + core},
            device_id_type=MESH,
        )

    for p in range(PHASES):
        own_copy(p).start()
    dn_copy.start()

    barrier = pltpu.get_barrier_semaphore()
    for k in range(1, n_ad):
        pl.semaphore_signal(barrier, inc=1, device_id=ad_peer(k), device_id_type=MESH)
    for k in range(1, n_tp):
        pl.semaphore_signal(barrier, inc=1, device_id=tp_peer(k), device_id_type=MESH)
    for j in range(CHUNKS):
        w_copy(j).start()
    up_copy.start()

    own_ids = ids[...]
    own_slots = jnp.zeros(own_ids.shape, F32)
    for a in range(table.shape[0]):
        own_slots = jnp.where(own_ids == a, table[a].astype(F32), own_slots)
    own_slots = jnp.broadcast_to(own_slots, (8, rows_dev)).astype(BF16)
    source = lax.broadcasted_iota(jnp.int32, (rows_dev, rows), 0)
    lane = lax.broadcasted_iota(jnp.int32, (rows_dev, rows), 1)
    for p in range(PHASES):
        inside = jnp.logical_and(source >= p * hp, source < (p + 1) * hp)
        place = jnp.logical_and(inside, lane == me_ad * hp + source - p * hp)
        onehot = jnp.where(place, 1.0, 0.0).astype(BF16)
        meta_own[p] = jnp.dot(own_slots, onehot, preferred_element_type=F32)

    pl.semaphore_wait(barrier, n_ad + n_tp - 2)
    for k in range(1, n_ad):
        m_copy(k).start()
    for k in range(1, n_ad):
        x_send(0, k).start()
    for k in range(1, n_ad):
        m_copy(k).wait_recv()
    for p in range(PHASES):
        total = meta_own[p]
        for k in range(1, n_ad):
            total += meta_in[k - 1, p]
        slots[p] = total
        slot_row = total[0:1]
        scale_row = jnp.zeros((1, rows), F32)
        for s in range(n_slots):
            scale_row = jnp.where(slot_row == float(s), scales[s], scale_row)
        scale_cols[p] = jnp.broadcast_to(scale_row, (128, rows)).T
    dn_copy.wait()

    def base(p, first, last):
        @pl.loop(first, last)
        def _(j):
            if p == 0:
                w_copy(j).wait()

            @pl.loop(0, cw // tile)
            def _(i):
                at = pl.ds(pl.multiple_of(j * cw + i * tile, tile), tile)
                acc[:, at] = jnp.dot(x_all[p], w[:, at], preferred_element_type=F32)

    def forward(p, j):
        s1_copy(p, j).wait_recv()
        for k in range(1, n_x):
            at = lax.rem(me_x + k, n_x)
            both = keep[p, j, at].astype(F32) + recv1[p, j, at].astype(F32)
            send2[p, j, k - 1] = both.astype(BF16)
            s2_copy(p, j, k).start()

    def finish(p):
        @pl.loop(0, CHUNKS)
        def _(j):
            total = keep[p, j, me_x].astype(F32) + recv1[p, j, me_x].astype(F32)
            for k in range(1, n_x):
                s2_copy(p, j, k).wait_recv()
                total += recv2[p, j, k - 1].astype(F32)
            total = total.astype(BF16)
            for b in range(blocks):
                out[pl.ds(b * rows_dev + p * hp, hp), cols(j)] = total[b * hp : (b + 1) * hp]

    for p in range(PHASES):
        own_copy(p).wait()
        for k in range(1, n_ad):
            x_recv(p, k).wait_recv()
        if p + 1 < PHASES:
            for k in range(1, n_ad):
                x_send(p, k).wait_send()
            for k in range(1, n_ad):
                x_send(p + 1, k).start()

        slot_row = slots[p][0:1]
        partial = lax.dot_general(
            dn[...], x_all[p], (((1,), (1,)), ((), ())), preferred_element_type=F32
        )
        mine = jnp.zeros((rank, rows), F32)
        for h in range(owned):
            here = (me_ad * owned + h).astype(F32)
            mine = jnp.where(slot_row == here, partial[h * rank : (h + 1) * rank], mine)
        for t in range(n_tp):
            a_send[p, t] = mine[t * rank_part : (t + 1) * rank_part]
        for k in range(1, n_tp):
            a_copy(p, k).start()

        base(p, 0, EARLY)

        total = a_send[p, me_tp]
        for k in range(1, n_tp):
            a_copy(p, k).wait_recv()
            total += a_recv[p, k - 1]
        b_send[p] = total.astype(BF16).astype(F32)
        for k in range(1, n_ad):
            b_copy(p, k).start()

        base(p, EARLY, CHUNKS)

        shrunk = b_send[p]
        for k in range(1, n_ad):
            b_copy(p, k).wait_recv()
            shrunk += b_recv[p, k - 1]
        for s in range(n_slots):
            spread[pl.ds(s * rank_part, rank_part)] = jnp.where(slot_row == float(s), shrunk, 0.0)
        expand[...] = spread[...].T.astype(BF16)
        if p == 0:
            up_copy.wait()

        @pl.loop(0, CHUNKS)
        def _(j):
            delta = jnp.dot(expand[...], upv[:, cols(j)], preferred_element_type=F32)
            term = acc[:, cols(j)] + scale_cols[p][:, 0:1] * delta
            term = term.astype(BF16)
            for x in range(n_x):
                even = term[2 * x * per_dest : (2 * x + 1) * per_dest]
                odd = term[(2 * x + 1) * per_dest : (2 * x + 2) * per_dest]
                send1[p, j, x] = jnp.where(core == 0, odd, even)
                keep[p, j, x] = jnp.where(core == 0, even, odd)
            s1_copy(p, j).start()

            @pl.when(j > 0)
            def _():
                forward(p, j - 1)

        forward(p, CHUNKS - 1)

    for p in range(PHASES):
        finish(p)

    for k in range(1, n_ad):
        m_copy(k).wait_send()
        x_send(PHASES - 1, k).wait_send()
    for p in range(PHASES):
        for k in range(1, n_tp):
            a_copy(p, k).wait_send()
        for k in range(1, n_ad):
            b_copy(p, k).wait_send()

        @pl.loop(0, CHUNKS)
        def _(j):
            s1_copy(p, j).wait_send()
            for k in range(1, n_x):
                s2_copy(p, j, k).wait_send()


def per_device(
    tokens,
    row_adapter_index,
    adapter_slot_table,
    gate_matrix,
    down_weight_slots,
    up_weight_slots,
    slot_scale_table,
):
    n_ad = lax.axis_size("ad")
    n_tp = lax.axis_size("tp")
    rows_dev, depth = tokens.shape
    width = gate_matrix.shape[1]
    owned, rank, _ = down_weight_slots.shape
    n_slots, rank_part, _ = up_weight_slots.shape
    hp = rows_dev // PHASES
    rows = n_ad * hp
    n_x = n_tp // 2
    per_dest = rows // n_tp
    cw = width // CHUNKS
    out_rows = rows_dev * n_ad // n_tp
    vmem = pl.BlockSpec(memory_space=pltpu.VMEM)
    smem = pl.BlockSpec(memory_space=pltpu.SMEM)
    hbm = pl.BlockSpec(memory_space=pl.ANY)
    dma = pltpu.SemaphoreType.DMA
    return pl.pallas_call(
        functools.partial(kernel, n_ad, n_tp),
        out_shape=jax.ShapeDtypeStruct((out_rows, width), BF16),
        in_specs=[hbm, vmem, smem, smem, hbm, hbm, hbm],
        out_specs=vmem,
        scratch_shapes=[
            pltpu.VMEM((PHASES, rows, depth), BF16),
            pltpu.VMEM((depth, width), BF16),
            pltpu.VMEM((owned * rank, depth), BF16),
            pltpu.VMEM((n_slots * rank_part, width), BF16),
            pltpu.VMEM((rows, width), F32),
            pltpu.VMEM((PHASES, 8, rows), F32),
            pltpu.VMEM((n_ad - 1, PHASES, 8, rows), F32),
            pltpu.VMEM((PHASES, 8, rows), F32),
            pltpu.VMEM((PHASES, rows, 128), F32),
            pltpu.VMEM((PHASES, n_tp, rank_part, rows), F32),
            pltpu.VMEM((PHASES, n_tp - 1, rank_part, rows), F32),
            pltpu.VMEM((PHASES, rank_part, rows), F32),
            pltpu.VMEM((PHASES, n_ad - 1, rank_part, rows), F32),
            pltpu.VMEM((n_slots * rank_part, rows), F32),
            pltpu.VMEM((rows, n_slots * rank_part), BF16),
            pltpu.VMEM((PHASES, CHUNKS, n_x, per_dest, cw), BF16),
            pltpu.VMEM((PHASES, CHUNKS, n_x, per_dest, cw), BF16),
            pltpu.VMEM((PHASES, CHUNKS, n_x, per_dest, cw), BF16),
            pltpu.VMEM((PHASES, CHUNKS, n_x - 1, per_dest, cw), BF16),
            pltpu.VMEM((PHASES, CHUNKS, n_x - 1, per_dest, cw), BF16),
            dma((CHUNKS,)),
            dma((2 + PHASES,)),
            dma((PHASES, n_ad - 1)),
            dma((PHASES, n_ad - 1)),
            dma((n_ad - 1,)),
            dma((n_ad - 1,)),
            dma((PHASES, n_tp - 1)),
            dma((PHASES, n_tp - 1)),
            dma((PHASES, n_ad - 1)),
            dma((PHASES, n_ad - 1)),
            dma((PHASES, CHUNKS)),
            dma((PHASES, CHUNKS)),
            dma((PHASES, CHUNKS, n_x - 1)),
            dma((PHASES, CHUNKS, n_x - 1)),
        ],
        compiler_params=pltpu.CompilerParams(
            collective_id=0, has_side_effects=True, vmem_limit_bytes=60 * 1024 * 1024
        ),
    )(
        tokens,
        row_adapter_index.reshape(1, rows_dev),
        adapter_slot_table,
        slot_scale_table,
        gate_matrix,
        down_weight_slots.reshape(owned * rank, depth),
        up_weight_slots.reshape(n_slots * rank_part, width),
    )


def solution(mesh):
    in_specs = (
        P(("grp", "ad"), "tp"),
        P(("grp", "ad")),
        P("grp"),
        P("tp", "ad"),
        P("ad", None, "tp"),
        P(None, "tp", "ad"),
        P(),
    )
    out_specs = P(("grp", "tp"), "ad")
    return jax.shard_map(
        per_device, mesh=mesh, in_specs=in_specs, out_specs=out_specs, check_vma=False
    )
```

time: 138 us -> 68.1 us (0.49)
  Pallas kernels: 0 us -> 65.8 us
  waiting for transfers between devices: 52.3 us -> 0 us
  blocking collectives: 32.5 us -> 0 us
  matrix products: 25.3 us -> 0 us
  between operations: 14.2 us -> 0.01 us
  local copies, waits for them, and re-layouts: 10.5 us -> 2.16 us
  other arithmetic: 3.04 us -> 0 us
    pallas_call x0 -> x1, Pallas kernels: none -> 65.8 us  [per_device(): pl.pallas_call(functools.partial(kernel, n_ad, n_tp), out_shape=jax.Shape...]
    reduce_scatter x1 -> x0, waiting for transfers between devices: 39.4 us -> none  [per_device(): lax.psum_scatter(terms.astype(jnp.bfloat16), 'tp', scatter_dimension=0, t...]
    dot_general x3 -> x0, matrix products: 25.3 us -> none  [the longest x1 19.8 us: per_device(): jnp.dot(gathered, gate_matrix, preferred_element_type=jnp.float32)]
    all_gather x1 -> x0, waiting for transfers between devices: 12.2 us -> none  [per_device(): lax.all_gather(tokens, 'ad', axis=0, tiled=True)]
    all_gather x1 -> x0, blocking collectives: 11.9 us -> none  [per_device(): all_ranks = lax.all_gather(rank_piece, 'ad', axis=1, tiled=True)]
    psum x1 -> x0, blocking collectives: 10.8 us -> none  [per_device(): lax.psum(owner_terms.astype(jnp.bfloat16), 'tp').astype(jnp.float32)]
    unnamed x1 -> x0, blocking collectives: 9.89 us -> none
    gather x3 -> x0, local copies, waits for them, and re-layouts: 5.01 us -> none  [the longest x1 2.89 us: per_device(): selected_rows = gathered[picked]]
  transfers between devices with their start and end apart: 2 -> 0, of which waited for: 2 -> 0; matrix products, arithmetic and copies ran while one was open for 7% -> 0% of each run, Pallas kernels for 0% -> 0%
where the time goes in v1:
time: 68.1 us; the launch traced here: 68 us
  Pallas kernels  65.8 us (97%)
  local copies, waits for them, and re-layouts  2.16 us (3%)
    pallas_call x1, Pallas kernels, per_device(): pl.pallas_call(functools.partial(kernel, n_ad, n_tp), out_shape=jax.Shape...  65.8 us
    unnamed x1, local copies, waits for them, and re-layouts  2.16 us

profile of v1, /device:TPU:0, one launch (start us, length us, event | category | flops | bytes accessed | tf_op | source)
XLA Modules:
  0.0 68.0 jit_solution(13468913448310608282)
XLA Ops:
  0.0 65.8 %shard_map.73 = bf16[64,7168]{1,0:T(8,128)(2,1)} custom-call(bf16[64,2048]{1,0:T(8,128)(2,1)} %tokens.1, s32[1,64]{1,0:T(1,128)} %bitcast.5, s32[8]{0:T(128)} %table.1, f32[8]{0:T(128)} %scales.1, bf16[2048,7168]{1,0:T(8,128)(2,1)} %gate.1, bf16[128,2048]{1,0:T(8,128)(2,1)} %bitcast.4, bf16[128,7168]{1,0:T(8,128)(2,1)} %bitcast.3), custom_call_target="tpu_custom_call" | custom-call | tf_op jit(solution)/shard_map/pallas_call | solution.py:357
  65.8 2.2 %copy.9 = bf16[64,7168]{1,0:T(8,128)(2,1)} copy(bf16[64,7168]{1,0:T(8,128)(2,1)} %shard_map.73) | data formatting | bytes 1835008

commit v2 on v1

--- a/solution.py
+++ b/solution.py
@@ -9,7 +9,6 @@
 
 PHASES = 2
 CHUNKS = 7
-EARLY = 3
 MESH = pl.DeviceIdType.MESH
 F32 = jnp.float32
 BF16 = jnp.bfloat16
@@ -70,7 +69,7 @@
     hp = rows_dev // PHASES
     rows = n_ad * hp
     cw = gate.shape[1] // CHUNKS
-    tile = 256 if cw % 256 == 0 else cw
+    tile = 512 if cw % 512 == 0 else cw
     rank_part = a_recv.shape[2]
     rank = rank_part * n_tp
     owned = down.shape[0] // rank
@@ -101,26 +100,43 @@
             tokens.at[pl.ds(p * hp, hp)], own_rows(p), local_sem.at[2 + p]
         )
 
-    def x_send(p, k):
-        return pltpu.make_async_remote_copy(
-            src_ref=tokens.at[pl.ds(p * hp, hp)],
-            dst_ref=own_rows(p),
-            send_sem=x_ssem.at[p, k - 1],
-            recv_sem=x_rsem.at[p, k - 1],
-            device_id=ad_peer(k),
-            device_id_type=MESH,
-        )
-
-    def x_recv(p, k):
-        origin = lax.rem(me_ad + n_ad - k, n_ad)
-        return pltpu.make_async_remote_copy(
-            src_ref=tokens.at[pl.ds(p * hp, hp)],
-            dst_ref=x_all.at[p, pl.ds(pl.multiple_of(origin * hp, hp), hp)],
-            send_sem=x_ssem.at[p, k - 1],
-            recv_sem=x_rsem.at[p, k - 1],
-            device_id=ad_peer(k),
-            device_id_type=MESH,
-        )
+    def hop(p, s, way, block):
+        block = lax.rem(block + n_ad, n_ad)
+        at = pl.ds(pl.multiple_of(block * hp, hp), hp)
+        return pltpu.make_async_remote_copy(
+            src_ref=tokens.at[pl.ds(p * hp, hp)] if s == 1 else x_all.at[p, at],
+            dst_ref=x_all.at[p, at],
+            send_sem=x_ssem.at[p, (1 - way) // 2, s - 1],
+            recv_sem=x_rsem.at[p, (1 - way) // 2, s - 1],
+            device_id={"ad": lax.rem(me_ad + way + n_ad, n_ad)},
+            device_id_type=MESH,
+        )
+
+    def sends(s, way):
+        if way > 0:
+            return jnp.logical_and(me_ad < n_ad - 1, me_ad >= s - 1)
+        return jnp.logical_and(me_ad > 0, me_ad <= n_ad - s)
+
+    def hop_start(p, s):
+        for way in (1, -1):
+
+            @pl.when(sends(s, way))
+            def _():
+                hop(p, s, way, me_ad - way * (s - 1)).start()
+
+    def hop_sent(p, s):
+        for way in (1, -1):
+
+            @pl.when(sends(s, way))
+            def _():
+                hop(p, s, way, me_ad - way * (s - 1)).wait_send()
+
+    def hop_recv(p, s):
+        for way in (1, -1):
+
+            @pl.when(me_ad >= s if way > 0 else me_ad <= n_ad - 1 - s)
+            def _():
+                hop(p, s, way, me_ad - way * s).wait_recv()
 
     def m_copy(k):
         return pltpu.make_async_remote_copy(
@@ -152,12 +168,13 @@
             device_id_type=MESH,
         )
 
-    def s1_copy(p, j):
-        return pltpu.make_async_remote_copy(
-            src_ref=send1.at[p, j],
-            dst_ref=recv1.at[p, j],
-            send_sem=s1_ssem.at[p, j],
-            recv_sem=s1_rsem.at[p, j],
+    def s1_copy(p, j, k):
+        at = lax.rem(me_x + k, n_x)
+        return pltpu.make_async_remote_copy(
+            src_ref=send1.at[p, j, at],
+            dst_ref=recv1.at[p, j, at],
+            send_sem=s1_ssem.at[p, j, k],
+            recv_sem=s1_rsem.at[p, j, k],
             device_id={"tp": me_x * 2 + 1 - core},
             device_id_type=MESH,
         )
@@ -201,8 +218,7 @@
     pl.semaphore_wait(barrier, n_ad + n_tp - 2)
     for k in range(1, n_ad):
         m_copy(k).start()
-    for k in range(1, n_ad):
-        x_send(0, k).start()
+    hop_start(0, 1)
     for k in range(1, n_ad):
         m_copy(k).wait_recv()
     for p in range(PHASES):
@@ -217,46 +233,35 @@
         scale_cols[p] = jnp.broadcast_to(scale_row, (128, rows)).T
     dn_copy.wait()
 
-    def base(p, first, last):
-        @pl.loop(first, last)
-        def _(j):
-            if p == 0:
-                w_copy(j).wait()
-
-            @pl.loop(0, cw // tile)
-            def _(i):
-                at = pl.ds(pl.multiple_of(j * cw + i * tile, tile), tile)
-                acc[:, at] = jnp.dot(x_all[p], w[:, at], preferred_element_type=F32)
+    def base(p, j):
+        if p == 0:
+            w_copy(j).wait()
+
+        @pl.loop(0, cw // tile)
+        def _(i):
+            at = pl.ds(pl.multiple_of(j * cw + i * tile, tile), tile)
+            acc[p, :, at] = jnp.dot(x_all[p], w[:, at], preferred_element_type=F32)
 
     def forward(p, j):
-        s1_copy(p, j).wait_recv()
         for k in range(1, n_x):
+            s1_copy(p, j, k).wait_recv()
             at = lax.rem(me_x + k, n_x)
             both = keep[p, j, at].astype(F32) + recv1[p, j, at].astype(F32)
             send2[p, j, k - 1] = both.astype(BF16)
             s2_copy(p, j, k).start()
 
-    def finish(p):
-        @pl.loop(0, CHUNKS)
-        def _(j):
-            total = keep[p, j, me_x].astype(F32) + recv1[p, j, me_x].astype(F32)
-            for k in range(1, n_x):
-                s2_copy(p, j, k).wait_recv()
-                total += recv2[p, j, k - 1].astype(F32)
-            total = total.astype(BF16)
-            for b in range(blocks):
-                out[pl.ds(b * rows_dev + p * hp, hp), cols(j)] = total[b * hp : (b + 1) * hp]
-
-    for p in range(PHASES):
+    def finish(p, j):
+        s1_copy(p, j, 0).wait_recv()
+        total = keep[p, j, me_x].astype(F32) + recv1[p, j, me_x].astype(F32)
+        for k in range(1, n_x):
+            s2_copy(p, j, k).wait_recv()
+            total += recv2[p, j, k - 1].astype(F32)
+        total = total.astype(BF16)
+        for b in range(blocks):
+            out[pl.ds(b * rows_dev + p * hp, hp), cols(j)] = total[b * hp : (b + 1) * hp]
+
+    def shrink(p):
         own_copy(p).wait()
-        for k in range(1, n_ad):
-            x_recv(p, k).wait_recv()
-        if p + 1 < PHASES:
-            for k in range(1, n_ad):
-                x_send(p, k).wait_send()
-            for k in range(1, n_ad):
-                x_send(p + 1, k).start()
-
         slot_row = slots[p][0:1]
         partial = lax.dot_general(
             dn[...], x_all[p], (((1,), (1,)), ((), ())), preferred_element_type=F32
@@ -270,8 +275,7 @@
         for k in range(1, n_tp):
             a_copy(p, k).start()
 
-        base(p, 0, EARLY)
-
+    def share(p):
         total = a_send[p, me_tp]
         for k in range(1, n_tp):
             a_copy(p, k).wait_recv()
@@ -280,43 +284,91 @@
         for k in range(1, n_ad):
             b_copy(p, k).start()
 
-        base(p, EARLY, CHUNKS)
-
+    def widen(p):
+        slot_row = slots[p][0:1]
         shrunk = b_send[p]
         for k in range(1, n_ad):
             b_copy(p, k).wait_recv()
             shrunk += b_recv[p, k - 1]
         for s in range(n_slots):
             spread[pl.ds(s * rank_part, rank_part)] = jnp.where(slot_row == float(s), shrunk, 0.0)
-        expand[...] = spread[...].T.astype(BF16)
-        if p == 0:
-            up_copy.wait()
-
-        @pl.loop(0, CHUNKS)
-        def _(j):
-            delta = jnp.dot(expand[...], upv[:, cols(j)], preferred_element_type=F32)
-            term = acc[:, cols(j)] + scale_cols[p][:, 0:1] * delta
-            term = term.astype(BF16)
-            for x in range(n_x):
-                even = term[2 * x * per_dest : (2 * x + 1) * per_dest]
-                odd = term[(2 * x + 1) * per_dest : (2 * x + 2) * per_dest]
-                send1[p, j, x] = jnp.where(core == 0, odd, even)
-                keep[p, j, x] = jnp.where(core == 0, even, odd)
-            s1_copy(p, j).start()
-
-            @pl.when(j > 0)
-            def _():
-                forward(p, j - 1)
-
-        forward(p, CHUNKS - 1)
-
-    for p in range(PHASES):
-        finish(p)
+        expand[p] = spread[...].T.astype(BF16)
+
+    def term(p, j):
+        delta = jnp.dot(expand[p], upv[:, cols(j)], preferred_element_type=F32)
+        value = acc[p, :, cols(j)] + scale_cols[p][:, 0:1] * delta
+        value = value.astype(BF16)
+        for x in range(n_x):
+            even = value[2 * x * per_dest : (2 * x + 1) * per_dest]
+            odd = value[(2 * x + 1) * per_dest : (2 * x + 2) * per_dest]
+            send1[p, j, x] = jnp.where(core == 0, odd, even)
+            keep[p, j, x] = jnp.where(core == 0, even, odd)
+        for k in list(range(1, n_x)) + [0]:
+            s1_copy(p, j, k).start()
+
+    for s in range(1, n_ad):
+        if s > 1:
+            hop_start(0, s)
+        hop_recv(0, s)
+    hop_start(1, 1)
+    shrink(0)
+    pl.loop(0, 2)(lambda j: base(0, j))
+    share(0)
+    half = n_ad // 2
+    for s in range(1, half):
+        hop_recv(1, s)
+        hop_start(1, s + 1)
+    pl.loop(2, 5)(lambda j: base(0, j))
+    for s in range(half, n_ad - 1):
+        hop_recv(1, s)
+        hop_start(1, s + 1)
+    up_copy.wait()
+    widen(0)
+
+    @pl.loop(0, 2)
+    def _(j):
+        term(0, j)
+        base(0, j + 5)
+        forward(0, j)
+
+    term(0, 2)
+    hop_recv(1, n_ad - 1)
+    shrink(1)
+    forward(0, 2)
+
+    @pl.loop(3, 7)
+    def _(j):
+        term(0, j)
+        base(1, j - 3)
+
+        @pl.when(j == 4)
+        def _():
+            share(1)
+
+        forward(0, j)
+
+    widen(1)
+
+    @pl.loop(0, 3)
+    def _(j):
+        term(1, j)
+        base(1, j + 4)
+        forward(1, j)
+        finish(0, j)
+
+    @pl.loop(3, 7)
+    def _(j):
+        term(1, j)
+        finish(0, j)
+        forward(1, j)
+
+    pl.loop(0, CHUNKS)(lambda j: finish(1, j))
 
     for k in range(1, n_ad):
         m_copy(k).wait_send()
-        x_send(PHASES - 1, k).wait_send()
     for p in range(PHASES):
+        for s in range(1, n_ad):
+            hop_sent(p, s)
         for k in range(1, n_tp):
             a_copy(p, k).wait_send()
         for k in range(1, n_ad):
@@ -324,7 +376,8 @@
 
         @pl.loop(0, CHUNKS)
         def _(j):
-            s1_copy(p, j).wait_send()
+            for k in range(n_x):
+                s1_copy(p, j, k).wait_send()
             for k in range(1, n_x):
                 s2_copy(p, j, k).wait_send()
 
@@ -364,7 +417,7 @@
             pltpu.VMEM((depth, width), BF16),
             pltpu.VMEM((owned * rank, depth), BF16),
             pltpu.VMEM((n_slots * rank_part, width), BF16),
-            pltpu.VMEM((rows, width), F32),
+            pltpu.VMEM((PHASES, rows, width), F32),
             pltpu.VMEM((PHASES, 8, rows), F32),
             pltpu.VMEM((n_ad - 1, PHASES, 8, rows), F32),
             pltpu.VMEM((PHASES, 8, rows), F32),
@@ -374,7 +427,7 @@
             pltpu.VMEM((PHASES, rank_part, rows), F32),
             pltpu.VMEM((PHASES, n_ad - 1, rank_part, rows), F32),
             pltpu.VMEM((n_slots * rank_part, rows), F32),
-            pltpu.VMEM((rows, n_slots * rank_part), BF16),
+            pltpu.VMEM((PHASES, rows, n_slots * rank_part), BF16),
             pltpu.VMEM((PHASES, CHUNKS, n_x, per_dest, cw), BF16),
             pltpu.VMEM((PHASES, CHUNKS, n_x, per_dest, cw), BF16),
             pltpu.VMEM((PHASES, CHUNKS, n_x, per_dest, cw), BF16),
@@ -382,16 +435,16 @@
             pltpu.VMEM((PHASES, CHUNKS, n_x - 1, per_dest, cw), BF16),
             dma((CHUNKS,)),
             dma((2 + PHASES,)),
-            dma((PHASES, n_ad - 1)),
-            dma((PHASES, n_ad - 1)),
+            dma((PHASES, 2, n_ad - 1)),
+            dma((PHASES, 2, n_ad - 1)),
             dma((n_ad - 1,)),
             dma((n_ad - 1,)),
             dma((PHASES, n_tp - 1)),
             dma((PHASES, n_tp - 1)),
             dma((PHASES, n_ad - 1)),
             dma((PHASES, n_ad - 1)),
-            dma((PHASES, CHUNKS)),
-            dma((PHASES, CHUNKS)),
+            dma((PHASES, CHUNKS, n_x)),
+            dma((PHASES, CHUNKS, n_x)),
             dma((PHASES, CHUNKS, n_x - 1)),
             dma((PHASES, CHUNKS, n_x - 1)),
         ],

time: 68.1 us -> 57.4 us (0.84)
  Pallas kernels: 65.8 us -> 55.1 us
    pallas_call x1, Pallas kernels: 65.8 us -> 55.1 us  [per_device(): pl.pallas_call(functools.partial(kernel, n_ad, n_tp), out_shape=jax.Shape...]
where the time goes in v2:
time: 57.4 us; the launch traced here: 57.3 us
  Pallas kernels  55.1 us (96%)
  local copies, waits for them, and re-layouts  2.16 us (4%)
    pallas_call x1, Pallas kernels, per_device(): pl.pallas_call(functools.partial(kernel, n_ad, n_tp), out_shape=jax.Shape...  55.1 us
    unnamed x1, local copies, waits for them, and re-layouts  2.16 us

profile of v2, /device:TPU:0, one launch (start us, length us, event | category | flops | bytes accessed | tf_op | source)
XLA Modules:
  0.0 57.3 jit_solution(3114466571471986553)
XLA Ops:
  0.0 55.1 %shard_map.73 = bf16[64,7168]{1,0:T(8,128)(2,1)} custom-call(bf16[64,2048]{1,0:T(8,128)(2,1)} %tokens.1, s32[1,64]{1,0:T(1,128)} %bitcast.5, s32[8]{0:T(128)} %table.1, f32[8]{0:T(128)} %scales.1, bf16[2048,7168]{1,0:T(8,128)(2,1)} %gate.1, bf16[128,2048]{1,0:T(8,128)(2,1)} %bitcast.4, bf16[128,7168]{1,0:T(8,128)(2,1)} %bitcast.3), custom_call_target="tpu_custom_call" | custom-call | tf_op jit(solution)/shard_map/pallas_call | solution.py:410
  55.1 2.2 %copy.9 = bf16[64,7168]{1,0:T(8,128)(2,1)} copy(bf16[64,7168]{1,0:T(8,128)(2,1)} %shard_map.73) | data formatting | bytes 1835008

commit v3 on v2

--- a/solution.py
+++ b/solution.py
@@ -309,8 +309,9 @@
     for s in range(1, n_ad):
         if s > 1:
             hop_start(0, s)
+        if s == n_ad - 1:
+            hop_start(1, 1)
         hop_recv(0, s)
-    hop_start(1, 1)
     shrink(0)
     pl.loop(0, 2)(lambda j: base(0, j))
     share(0)

time: 57.4 us -> 55.1 us (0.960)
  Pallas kernels: 55.1 us -> 52.8 us
    pallas_call x1, Pallas kernels: 55.1 us -> 52.8 us  [per_device(): pl.pallas_call(functools.partial(kernel, n_ad, n_tp), out_shape=jax.Shape...]
where the time goes in v3:
time: 55.1 us; the launch traced here: 54.9 us
  Pallas kernels  52.8 us (96%)
  local copies, waits for them, and re-layouts  2.16 us (4%)
    pallas_call x1, Pallas kernels, per_device(): pl.pallas_call(functools.partial(kernel, n_ad, n_tp), out_shape=jax.Shape...  52.8 us
    unnamed x1, local copies, waits for them, and re-layouts  2.16 us

profile of v3, /device:TPU:0, one launch (start us, length us, event | category | flops | bytes accessed | tf_op | source)
XLA Modules:
  0.0 54.9 jit_solution(18083259638221616930)
XLA Ops:
  0.0 52.8 %shard_map.73 = bf16[64,7168]{1,0:T(8,128)(2,1)} custom-call(bf16[64,2048]{1,0:T(8,128)(2,1)} %tokens.1, s32[1,64]{1,0:T(1,128)} %bitcast.5, s32[8]{0:T(128)} %table.1, f32[8]{0:T(128)} %scales.1, bf16[2048,7168]{1,0:T(8,128)(2,1)} %gate.1, bf16[128,2048]{1,0:T(8,128)(2,1)} %bitcast.4, bf16[128,7168]{1,0:T(8,128)(2,1)} %bitcast.3), custom_call_target="tpu_custom_call" | custom-call | tf_op jit(solution)/shard_map/pallas_call | solution.py:411
  52.8 2.2 %copy.9 = bf16[64,7168]{1,0:T(8,128)(2,1)} copy(bf16[64,7168]{1,0:T(8,128)(2,1)} %shard_map.73) | data formatting | bytes 1835008
